TPU v7x, 32 devices: a whole 2x2x4 slice. The times are simulated.
32 devices in a mesh: guide: 2 (over x), seq: 8 (over z, core), blk: 2 (over y).
Axes of the slice: x: 2, y: 2, z: 4, core: 2. Of those that a mesh axis runs over, the one named last changes fastest.
Arguments:
- img_hidden: bfloat16 [2, 2, 512, 3072], P('guide', None, 'seq', 'blk'), may hold values from -6 to 6
- img_query: bfloat16 [2, 2, 512, 3072], P('guide', None, 'seq', 'blk')
- img_key: bfloat16 [2, 2, 512, 3072], P('guide', None, 'seq', 'blk')
- img_value: bfloat16 [2, 2, 512, 3072], P('guide', None, 'seq', 'blk'), may hold values from -6 to 6
- txt_key: bfloat16 [2, 2, 512, 3072], P('guide', None, 'seq', 'blk'), may hold values from -6 to 6
- txt_value: bfloat16 [2, 2, 512, 3072], P('guide', None, 'seq', 'blk'), may hold values from -6 to 6
- query_gain: float32 [128], replicated
- key_gain: float32 [2, 128], replicated
- gate: float32 [2, 2, 3072], P('guide', None, 'blk'), may hold values from -4 to 4
- proj_weight: bfloat16 [3072, 3072], P('blk'), may hold values from -0.15625 to 0.15625
- proj_bias: float32 [3072], P('blk'), may hold values from -3 to 3
- guidance: float32 [2], replicated, may hold values from 1.5 to 5
- text_len: int32 [2], replicated, may hold values from 1 to 512, as said below
- step_index: int32 [1], replicated, may hold values from 0 to 7
- latent: bfloat16 [2, 512, 3072], P('guide', 'seq', 'blk'), may hold values from -6 to 6
Outputs:
- guided: bfloat16 [2, 512, 3072], P('guide', 'seq', 'blk')
- next_state: bfloat16 [2, 512, 3072], P('guide', 'seq', 'blk')
Inputs may be any that keep to these rules, and one draw needn't show every extreme that they name: `text_len`: some prompt has all 512 text slots live.
All inputs are finite; a program needn't handle non-finite values.
Results may differ from a plain program's by a relative error of at most 0.0095.
Values may be sent and summed in bfloat16 or wider, within the bound.
A program may use at most 64 MiB of HBM per device.

v0:
```python
import jax
import jax.numpy as jnp
from jax import lax
from jax.sharding import PartitionSpec as P

HD = 128
GRID = 64
STEPS = 8


def rope_angles(positions):
    first = HD // 8
    second = (HD - first) // 2
    freqs = 10000.0 ** (-jnp.arange(0, second, 2).astype(jnp.float32) / second)
    rows = (positions // GRID).astype(jnp.float32)
    cols = (positions % GRID).astype(jnp.float32)
    zeros = jnp.zeros((positions.shape[0], first // 2), jnp.float32)
    return jnp.concatenate([zeros, rows[:, None] * freqs, cols[:, None] * freqs], -1)


def rotate(values, angles):
    pairs = values.reshape(values.shape[:-1] + (HD // 2, 2))
    cosine = jnp.cos(angles)[None, :, None, :]
    sine = jnp.sin(angles)[None, :, None, :]
    first = pairs[..., 0] * cosine - pairs[..., 1] * sine
    second = pairs[..., 0] * sine + pairs[..., 1] * cosine
    return jnp.stack([first, second], -1).reshape(values.shape)


def normed(values, gain_row):
    heads = values.astype(jnp.float32).reshape(
        values.shape[0], values.shape[1], values.shape[2] // HD, HD
    )
    return heads / jnp.sqrt(jnp.mean(heads * heads, -1, keepdims=True) + 1e-06) * gain_row


def shards(
    img_hidden,
    img_query,
    img_key,
    img_value,
    txt_key,
    txt_value,
    query_gain,
    key_gain,
    gate,
    proj_weight,
    proj_bias,
    guidance,
    text_len,
    step_index,
    latent,
):
    prompts = img_query.shape[1]
    img_here = img_query.shape[2]
    txt_here = txt_key.shape[2]
    width_here = img_query.shape[3]
    heads_here = width_here // HD
    slot_here = img_here + txt_here
    positions = lax.axis_index("seq") * img_here + jnp.arange(img_here)
    angles = rope_angles(positions)
    queries = rotate(normed(img_query[0], query_gain), angles).astype(jnp.bfloat16)
    keys_img = rotate(normed(img_key[0], key_gain[0]), angles).astype(jnp.bfloat16)
    keys_txt = normed(txt_key[0], key_gain[1]).astype(jnp.bfloat16)
    keys_local = jnp.concatenate([keys_txt, keys_img], 1).reshape(prompts, slot_here, width_here)
    values_local = jnp.concatenate([txt_value[0], img_value[0]], 1)
    running = jnp.full((prompts, img_here, heads_here), -1e30, jnp.float32)
    key_piece = lax.all_gather(keys_local, "seq", axis=1, tiled=True)
    value_piece = lax.all_gather(values_local, "seq", axis=1, tiled=True)
    count = key_piece.shape[1]
    index = jnp.arange(count)
    device = index // slot_here
    within = index % slot_here
    text_pos = device * txt_here + within
    live = (within >= txt_here)[None, :] | (text_pos[None, :] < text_len[:, None])
    key_heads = key_piece.reshape(prompts, count, heads_here, HD)
    value_heads = value_piece.reshape(prompts, count, heads_here, HD)
    scores = jnp.einsum(
        "pqhd,pkhd->pqhk", queries, key_heads, preferred_element_type=jnp.float32
    ) * HD ** (-0.5)
    mask = live[:, None, None, :]
    scores = jnp.where(mask, scores, -1e30)
    newest = jnp.maximum(running, jnp.max(scores, -1))
    expo = jnp.where(mask, jnp.exp(scores - newest[..., None]), 0.0)
    total = jnp.sum(expo, -1)
    accum = jnp.einsum(
        "pqhk,pkhd->pqhd",
        expo.astype(jnp.bfloat16),
        value_heads,
        preferred_element_type=jnp.float32,
    )
    running, total, accum = (newest, total, accum)
    attn = (accum / total[..., None]).astype(jnp.bfloat16).reshape(prompts * img_here, width_here)
    partial_value = jnp.dot(attn, proj_weight, preferred_element_type=jnp.float32)
    proj = lax.psum_scatter(
        partial_value.astype(jnp.bfloat16), "blk", scatter_dimension=1, tiled=True
    ).astype(jnp.float32)
    proj = (proj + proj_bias).reshape(prompts, img_here, width_here)
    layer_out = (img_hidden[0].astype(jnp.float32) + gate[0][:, None, :] * proj).astype(
        jnp.bfloat16
    )
    both_halves = lax.all_to_all(layer_out[None], "guide", split_axis=1, concat_axis=0, tiled=True)
    cond = both_halves[0].astype(jnp.float32)
    uncond = both_halves[1].astype(jnp.float32)
    own_prompts = cond.shape[0]
    scale_here = lax.dynamic_slice_in_dim(
        guidance, lax.axis_index("guide") * own_prompts, own_prompts, 0
    )
    guided_f = uncond + scale_here[:, None, None] * (cond - uncond)
    index = step_index[0]
    u_now = 1.0 - index.astype(jnp.float32) / STEPS
    u_next = 1.0 - (index + 1).astype(jnp.float32) / STEPS
    step_size = 3.0 * u_next / (1.0 + 2.0 * u_next) - 3.0 * u_now / (1.0 + 2.0 * u_now)
    next_state = (latent.astype(jnp.float32) + step_size * guided_f).astype(jnp.bfloat16)
    return (guided_f.astype(jnp.bfloat16), next_state)


def solution(mesh):
    return jax.shard_map(
        shards,
        mesh=mesh,
        in_specs=(
            P("guide", None, "seq", "blk"),
            P("guide", None, "seq", "blk"),
            P("guide", None, "seq", "blk"),
            P("guide", None, "seq", "blk"),
            P("guide", None, "seq", "blk"),
            P("guide", None, "seq", "blk"),
            P(),
            P(),
            P("guide", None, "blk"),
            P("blk", None),
            P("blk"),
            P(),
            P(),
            P(),
            P("guide", "seq", "blk"),
        ),
        out_specs=(P("guide", "seq", "blk"), P("guide", "seq", "blk")),
        check_vma=False,
    )
```

profile of v0, /device:TPU:0, one launch (start us, length us, event | category | flops | bytes accessed | tf_op | source)
XLA Modules:
  0.0 215.6 jit_solution(14260598982114271699)
XLA Ops:
  7.2 2.0 convert_multiply_fusion.1
  9.3 1.3 copy.57
  10.5 2.0 convert_multiply_fusion.2
  12.5 1.3 copy.53
  13.8 0.1 mul.268
  14.0 2.3 %mul.267 = f32[2,64,12,128]{3,2,1,0:T(8,128)} reshape(f32[1,2,64,1536]{3,2,1,0:T(8,128)} %convert_multiply_fusion.2) | data formatting | bytes 1572864 | tf_op jit(solution)/shard_map/mul | solution.py:34
  16.2 1.6 reduce_sum.37
  17.9 0.1 copy.54
  17.9 2.3 %mul.285 = f32[2,64,12,128]{3,2,1,0:T(8,128)} reshape(f32[1,2,64,1536]{3,2,1,0:T(8,128)} %convert_multiply_fusion.1) | data formatting | bytes 1572864 | tf_op jit(solution)/shard_map/mul | solution.py:34
  20.2 1.6 reduce_sum.38
  21.8 0.1 copy.58
  21.9 0.1 mul.286
  22.1 0.1 broadcast_multiply_fusion.1
  22.1 0.2 fusion.29
  22.3 1.9 divide_multiply_fusion
  24.2 4.1 %subtract_convert_fusion = (bf16[2,64,12,64,1]{1,4,3,2,0:T(2,128)(2,1)S(1)}, bf16[2,64,12,64,1]{1,4,3,2,0:T(2,128)(2,1)S(1)}, bf16[2,64,12,64,1]{1,4,3,2,0:T(2,128)(2,1)S(1)}, bf16[2,64,12,64,1]{1,4,3,2,0:T(2,128)(2,1)S(1)}) fusion(f32[2,64,12,64,2]{1,4,3,2,0:T(2,128)S(1)} %get-tuple-element.20, f32[64,64]{0,1:T(8,128)S(1)} %get-tuple-element.11, ...), kind=kLoop, calls=%fused_computation.32 | loop fusion | flops 1572864 | bytes 2392064 | tf_op jit(solution)/shard_map/convert.5
  28.4 2.1 pad_maximum_fusion.1
  30.4 1.0 copy.55
  31.4 1.1 convert_multiply_fusion
  32.5 0.1 mul.260
  32.7 0.3 reduce_sum.36
  33.0 0.3 div.86
  33.4 0.1 div.87
  33.5 1.1 fusion.23
  34.6 2.0 pad_maximum_fusion.2
  36.7 0.0 all-gather.3.cloned.1.call-start
  36.7 1.4 copy.51
  38.1 1.4 copy.52
  39.5 1.3 pad_maximum_fusion
  40.8 0.2 reduce-scatter.2.cloned.1.call-start
  41.1 2.1 pad_maximum_fusion.3
  43.2 0.1 compare_or_fusion
  43.3 61.0 %all-gather.5.cloned.1.call-done = bf16[2,1024,1536]{2,1,0:T(8,128)(2,1)} async-done(((bf16[2,128,1536]{2,1,0:T(8,128)(2,1)}), bf16[2,1024,1536]{2,1,0:T(8,128)(2,1)}) %all-gather.5.cloned.1.call-update) | async-done | bytes 6291472 | tf_op jit(solution)/shard_map/all_gather | solution.py:68
  104.2 8.7 %copy.56 = bf16[2,1024,1536]{1,2,0:T(8,128)(2,1)} copy(bf16[2,1024,1536]{2,1,0:T(8,128)(2,1)} %all-gather.5.cloned.1.call-done) | data formatting | bytes 12582912 | tf_op jit(solution)/shard_map/all_gather | solution.py:68
  112.9 4.9 %bitcast_reduce_fusion = (f32[2,64,12]{1,2,0:T(8,128)S(1)}, f32[2,12,1024,64]{2,3,1,0:T(8,128)S(1)}) fusion(pred[2,1024]{1,0:T(4,128)(4,1)S(1)} %compare_or_fusion, bf16[2,1024,12,128]{1,3,2,0:T(8,128)(2,1)} %bitcast.82, bf16[2,64,12,128]{1,3,2,0:T(8,128)(2,1)S(1)} %bitcast.87), kind=kOutput, calls=%fused_computation.1 | convolution fusion | flops 407370240 | bytes 12984320 | tf_op jit(solution)/shard_map/pqhd,pkhd->pqhk/dot_general | solution.py:78
  117.9 2.6 %copy-done = f32[2,12,1024,64]{2,3,1,0:T(8,128)} copy-done((f32[2,12,1024,64]{2,3,1,0:T(8,128)}, f32[2,12,1024,64]{2,3,1,0:T(8,128)S(1)}, u32[]{:S(2)}) %copy-start) | copy-done | bytes 6291480
  120.5 1.8 fusion.2
  122.3 47.4 %all-gather.3.cloned.1.call-done = bf16[2,1024,1536]{1,2,0:T(8,128)(2,1)} async-done(((bf16[2,128,1536]{1,2,0:T(8,128)(2,1)}), bf16[2,1024,1536]{1,2,0:T(8,128)(2,1)}) %all-gather.3.cloned.1.call-update) | async-done | bytes 6291472 | tf_op jit(solution)/shard_map/all_gather | solution.py:69
  169.7 7.2 %fusion.18 = bf16[2,64,12,128]{3,1,2,0:T(8,128)(2,1)S(1)} fusion(bf16[2,1024,12,128]{1,3,2,0:T(8,128)(2,1)} %bitcast.95, f32[2,12,1024,64]{2,3,1,0:T(8,128)} %copy-done, f32[2,64,12]{1,2,0:T(8,128)S(1)} %broadcast_maximum_fusion, pred[2,1024]{1,0:T(4,128)(4,1)S(1)} %compare_or_fusion, f32[2,64,12]{1,2,0:T(8,128)S(1)} %fusion.2), kind=kOutput, calls=%fused_computation.21 | convolution fusion | flops 410910720 | bytes 12990464 | tf_op jit(solution)/shard_map/pqhk,pkhd->pqhd/dot_general | solution.py:86
  176.9 0.3 copy.62
  177.3 2.3 %convolution_convert_fusion = bf16[128,3072]{1,0:T(8,128)(2,1)} fusion(bf16[1536,3072]{1,0:T(8,128)(2,1)S(1)} %bitcast.84, bf16[16,8,12,128]{3,2,1,0:T(8,128)(2,1)S(1)} %bitcast.92), kind=kOutput, calls=%fused_computation.7 | convolution fusion | flops 1208352768 | bytes 10616832 | tf_op jit(solution)/shard_map/dot_general | solution.py:94
  179.6 15.8 %reduce-scatter.2.cloned.1.call-done = bf16[128,1536]{1,0:T(8,128)(2,1)} async-done(((bf16[128,3072]{1,0:T(8,128)(2,1)}), bf16[128,1536]{1,0:T(8,128)(2,1)}) %reduce-scatter.2.cloned.1.call-update) | async-done | bytes 393232 | tf_op jit(solution)/shard_map/reduce_scatter | solution.py:95
  195.4 1.1 convert_add_fusion
  196.5 0.8 add_convert_fusion
  197.4 3.5 %all-to-all-start = ((bf16[1,2,64,1536]{3,2,0,1:T(8,128)(2,1)}), bf16[1,2,64,1536]{3,2,0,1:T(8,128)(2,1)S(1)}, u32[]{:S(2)}, u32[]{:S(2)}) async-start(bf16[1,2,64,1536]{3,2,0,1:T(8,128)(2,1)} %add_convert_fusion), calls=%async_computation.1 | async-start | bytes 786432 | tf_op jit(solution)/shard_map/all_to_all | solution.py:102
  201.5 0.6 dynamic_slice.3
  202.2 5.5 %all-to-all-done = bf16[1,2,64,1536]{3,2,0,1:T(8,128)(2,1)S(1)} async-done(((bf16[1,2,64,1536]{3,2,0,1:T(8,128)(2,1)}), bf16[1,2,64,1536]{3,2,0,1:T(8,128)(2,1)S(1)}, u32[]{:S(2)}, u32[]{:S(2)}) %all-to-all-start) | async-done | bytes 393248 | tf_op jit(solution)/shard_map/all_to_all | solution.py:102
  207.6 1.4 add_convert_fusion.3
  (40 shorter events, 0.3 us)
Async XLA Ops:
  7.2 6.7 %copy-start.5 = (f32[2,128]{1,0:T(2,128)S(1)}, f32[2,128]{1,0:T(2,128)}, u32[]{:S(2)}) copy-start(f32[2,128]{1,0:T(2,128)} %param.22) | copy-start | bytes 3076
  7.2 97.1 %all-gather.5.cloned.1.call-start = ((), (), s32[]{:S(2)}) async-start(), calls=%async_computation.3 | async-start | bytes 7077888 | tf_op jit(solution)/shard_map/all_gather | solution.py:68
  7.2 14.6 %copy-start.6 = (f32[128]{0:T(128)S(1)}, f32[128]{0:T(128)}, u32[]{:S(2)}) copy-start(f32[128]{0:T(128)} %param.21) | copy-start | bytes 1540
  33.5 9.7 %copy-start.7 = (s32[2]{0:T(128)S(1)}, s32[2]{0:T(128)}, u32[]{:S(2)}) copy-start(s32[2]{0:T(128)} %param.27) | copy-start | bytes 28
  36.7 133.1 %all-gather.3.cloned.1.call-start = ((), (), s32[]{:S(2)}) async-start(), calls=%async_computation.2 | async-start | bytes 7077888 | tf_op jit(solution)/shard_map/all_gather | solution.py:69
  40.8 154.6 %reduce-scatter.2.cloned.1.call-start = ((), (), s32[]{:S(2)}) async-start(), calls=%async_computation.4 | async-start | bytes 1179648 | tf_op jit(solution)/shard_map/reduce_scatter | solution.py:95
  117.8 2.6 %copy-start = (f32[2,12,1024,64]{2,3,1,0:T(8,128)}, f32[2,12,1024,64]{2,3,1,0:T(8,128)S(1)}, u32[]{:S(2)}) copy-start(f32[2,12,1024,64]{2,3,1,0:T(8,128)S(1)} %get-tuple-element.17) | copy-start | bytes 18874372
  120.5 56.7 %slice-start = ((s8[9437184]{0:T(1024)(128)(4,1)}), s8[1048576]{0:T(1024)(128)(4,1)S(1)}, s32[]{:S(2)}) async-start(s8[9437184]{0:T(1024)(128)(4,1)} %bitcast.83), calls=%async_computation.5 | async-start | bytes 2097152
  169.7 7.5 %slice-start.1 = ((s8[9437184]{0:T(1024)(128)(4,1)}), s8[4194304]{0:T(1024)(128)(4,1)S(1)}, s32[]{:S(2)}) async-start(s8[9437184]{0:T(1024)(128)(4,1)} %bitcast.83), calls=%async_computation.6 | async-start | bytes 8388608
  169.7 7.5 %slice-start.2 = ((s8[9437184]{0:T(1024)(128)(4,1)}), s8[4194304]{0:T(1024)(128)(4,1)S(1)}, s32[]{:S(2)}) async-start(s8[9437184]{0:T(1024)(128)(4,1)} %bitcast.83), calls=%async_computation.7 | async-start | bytes 8388608
  177.3 18.2 %copy-start.4 = (f32[1536]{0:T(1024)S(1)}, f32[1536]{0:T(1024)}, u32[]{:S(2)}) copy-start(f32[1536]{0:T(1024)} %param.25) | copy-start | bytes 18436
  177.3 19.2 %copy-start.1 = (bf16[1,2,64,1536]{3,2,1,0:T(8,128)(2,1)S(1)}, bf16[1,2,64,1536]{3,2,1,0:T(8,128)(2,1)}, u32[]{:S(2)}) copy-start(bf16[1,2,64,1536]{3,2,1,0:T(8,128)(2,1)} %param.15) | copy-start | bytes 1179652
  177.3 19.2 %copy-start.3 = (f32[1,2,1536]{2,1,0:T(2,128)S(1)}, f32[1,2,1536]{2,1,0:T(2,128)}, u32[]{:S(2)}) copy-start(f32[1,2,1536]{2,1,0:T(2,128)} %param.23) | copy-start | bytes 36868
  177.3 24.2 %copy-start.8 = (f32[2]{0:T(128)S(1)}, f32[2]{0:T(128)}, u32[]{:S(2)}) copy-start(f32[2]{0:T(128)} %param.26) | copy-start | bytes 28
  177.3 30.3 %copy-start.2 = (bf16[1,64,1536]{2,1,0:T(8,128)(2,1)S(1)}, bf16[1,64,1536]{2,1,0:T(8,128)(2,1)}, u32[]{:S(2)}) copy-start(bf16[1,64,1536]{2,1,0:T(8,128)(2,1)} %param.29) | copy-start | bytes 589828
  197.4 10.3 %all-to-all-start = ((bf16[1,2,64,1536]{3,2,0,1:T(8,128)(2,1)}), bf16[1,2,64,1536]{3,2,0,1:T(8,128)(2,1)S(1)}, u32[]{:S(2)}, u32[]{:S(2)}) async-start(bf16[1,2,64,1536]{3,2,0,1:T(8,128)(2,1)} %add_convert_fusion), calls=%async_computation.1 | async-start | bytes 786432 | tf_op jit(solution)/shard_map/all_to_all | solution.py:102
Sparse Core Ops, SparseCore 0:
  36.8 67.4 all-gather.4
  105.8 63.8 all-gather.2
  179.8 15.6 reduce-scatter.1
where the time goes:
time: 217 us; the launch traced here: 216 us
  waiting for transfers between devices  130 us (60%)
  other arithmetic  28.7 us (13%)
  local copies, waits for them, and re-layouts  24 us (11%)
  between operations  14.9 us (7%)
  matrix products  14.4 us (7%)
  starting transfers between devices  3.77 us (2%)
    all_gather x1, waiting for transfers between devices, shards(): key_piece = lax.all_gather(keys_local, 'seq', axis=1, tiled=True)  61 us
    all_gather x1, waiting for transfers between devices, shards(): value_piece = lax.all_gather(values_local, 'seq', axis=1, tiled=True)  47.4 us
    reduce_scatter x1, waiting for transfers between devices, shards(): lax.psum_scatter(partial_value.astype(jnp.bfloat16), 'blk', scatter_dimen...  15.8 us
    all_gather x1, local copies, waits for them, and re-layouts, shards(): key_piece = lax.all_gather(keys_local, 'seq', axis=1, tiled=True)  8.67 us
    dot_general x1, matrix products, shards(): jnp.einsum('pqhk,pkhd->pqhd', expo.astype(jnp.bfloat16), value_heads, pre...  7.21 us
    all_to_all x1, waiting for transfers between devices, shards(): lax.all_to_all(layer_out[None], 'guide', split_axis=1, concat_axis=0, til...  5.46 us
    unnamed x26, local copies, waits for them, and re-layouts  5.43 us
    mul x3, other arithmetic, normed(): heads * heads  5.07 us
  transfers between devices with their start and end apart: 4, of which 4 were waited for; matrix products, arithmetic and copies ran while one was open for 10% of the time, Pallas kernels for 0%

commit v1 on v0

--- a/solution.py
+++ b/solution.py
@@ -1,6 +1,9 @@
 import jax
 import jax.numpy as jnp
+import numpy as np
 from jax import lax
+from jax.experimental import pallas as pl
+from jax.experimental.pallas import tpu as pltpu
 from jax.sharding import PartitionSpec as P
 
 HD = 128
@@ -115,9 +118,471 @@
     return (guided_f.astype(jnp.bfloat16), next_state)
 
 
+CHIPS = 4
+ROWS = 64
+CHUNKS = 4
+PER = 3
+UNITS = CHUNKS * PER
+HEADS_CORE = 6
+SCALE = HD ** (-0.5)
+F32 = jnp.float32
+BF16 = jnp.bfloat16
+
+
+def rope_table(devices):
+    first = HD // 8
+    second = (HD - first) // 2
+    freqs = (10000.0 ** (-np.arange(0, second, 2).astype(np.float32) / second)).astype(np.float32)
+    positions = np.arange(devices * ROWS)
+    rows = (positions // GRID).astype(np.float32)[:, None] * freqs
+    cols = (positions % GRID).astype(np.float32)[:, None] * freqs
+    angles = np.concatenate([np.zeros((positions.size, first // 2), np.float32), rows, cols], -1)
+    angles = np.repeat(angles, 2, -1)
+    table = np.concatenate([np.cos(angles), np.sin(angles)], -1).astype(np.float32)
+    return table.reshape(devices, ROWS, 2 * HD)
+
+
+def swap_matrix():
+    out = np.zeros((HD, HD), np.float32)
+    for pair in range(HD // 2):
+        out[2 * pair + 1, 2 * pair] = -1.0
+        out[2 * pair, 2 * pair + 1] = 1.0
+    return out
+
+
+def step_sizes():
+    def sigma(i):
+        u = 1.0 - i / STEPS
+        return 3.0 * u / (1.0 + 2.0 * u)
+
+    return [sigma(i + 1) - sigma(i) for i in range(STEPS)]
+
+
+def fused(
+    hid, q_in, ki_in, vi_in, kt_in, vt_in, qg, kg, gate, w_hbm, bias, guidance, tlen, sidx, latent,
+    rope_hbm, perm, guided_o, next_o,
+    weight, rope, q_all, keys, vals, vals_t, stage_q, stage_kv, part, lse, in_part, in_lse,
+    out_part, out_lse, own_t, attn, y_out, y_in, proj, x_out, x_in,
+    w_sem, rope_sem, ex_send, ex_recv, q_send, q_recv, p_send, p_recv, s_send, s_recv,
+    a_send, a_recv, y_send, y_recv, x_send, x_recv,
+):
+    g = lax.axis_index("guide")
+    s = lax.axis_index("seq")
+    b = lax.axis_index("blk")
+    z = s // 2
+    core = s % 2
+    other = 1 - core
+    peer = {"seq": 2 * z + other}
+    left = {"seq": s - 2}
+    right = {"seq": s + 2}
+    y_peer = {"blk": 1 - b}
+    x_peer = {"guide": 1 - g}
+    width = weight.shape[0]
+    half = width // 2
+    last = CHIPS - 1
+
+    def prompt_of(order):
+        return (1 - g) * (1 - order) + g * order
+
+    def remote(src, dst, send, recv, device):
+        return pltpu.make_async_remote_copy(
+            src_ref=src, dst_ref=dst, send_sem=send, recv_sem=recv,
+            device_id=device, device_id_type=pl.DeviceIdType.MESH,
+        )
+
+    barrier = pltpu.get_barrier_semaphore()
+
+    def greet(device):
+        pl.semaphore_signal(barrier, inc=1, device_id=device, device_id_type=pl.DeviceIdType.MESH)
+
+    greet(peer)
+    greet(y_peer)
+    greet(x_peer)
+    pl.when(z > 0)(lambda: greet(left))
+    pl.when(z < last)(lambda: greet(right))
+
+    w_copy = pltpu.make_async_copy(w_hbm, weight, w_sem)
+    w_copy.start()
+    rope_copy = pltpu.make_async_copy(rope_hbm.at[s], rope, rope_sem)
+    rope_copy.start()
+    rope_copy.wait()
+
+    lane = lax.broadcasted_iota(jnp.int32, (8, HD), 1)
+
+    def swapped(row):
+        wide = jnp.broadcast_to(row, (8, HD))
+        return jnp.where(
+            lane % 2 == 0, pltpu.roll(wide, HD - 1, 1), pltpu.roll(wide, 1, 1)
+        )[0:1]
+
+    def scaled(values):
+        return lax.rsqrt(jnp.mean(values * values, -1, keepdims=True) + 1e-06)
+
+    def roped(values, gain):
+        wide = values.astype(F32)
+        turned = jnp.dot(values, perm[...], preferred_element_type=F32)
+        cosine = rope[:, :HD] * gain
+        sine = rope[:, HD:] * swapped(gain)
+        return (scaled(wide) * (wide * cosine + turned * sine)).astype(BF16)
+
+    def plain(values, gain):
+        wide = values.astype(F32)
+        return (wide * scaled(wide) * gain).astype(BF16)
+
+    def each_chunk(step):
+        def run(chunk, carry):
+            step(chunk)
+            return carry
+
+        lax.fori_loop(0, CHUNKS, run, 0)
+
+    def place(chunk, i, owner):
+        order = chunk // 2
+        head = owner * HEADS_CORE + (chunk % 2) * PER + i
+        return prompt_of(order), pl.ds(pl.multiple_of(head * HD, HD), HD)
+
+    mine = pl.ds(pl.multiple_of(core * ROWS, ROWS), ROWS)
+    mine_img = pl.ds(pl.multiple_of((2 + core) * ROWS, ROWS), ROWS)
+    theirs = pl.ds(pl.multiple_of(other * ROWS, ROWS), ROWS)
+    theirs_img = pl.ds(pl.multiple_of((2 + other) * ROWS, ROWS), ROWS)
+
+    def queries_for_peer(chunk):
+        for i in range(PER):
+            p, cols = place(chunk, i, other)
+            stage_q[chunk * PER + i] = roped(q_in[0, p, :, cols], qg[...])
+
+    def queries_own(chunk):
+        for i in range(PER):
+            p, cols = place(chunk, i, core)
+            q_all[z, chunk * PER + i, mine, :] = roped(q_in[0, p, :, cols], qg[...])
+
+    def kv_for_peer(chunk):
+        for i in range(PER):
+            p, cols = place(chunk, i, other)
+            unit = chunk * PER + i
+            stage_kv[0, unit] = plain(kt_in[0, p, :, cols], kg[1:2])
+            stage_kv[1, unit] = roped(ki_in[0, p, :, cols], kg[0:1])
+            stage_kv[2, unit] = vt_in[0, p, :, cols]
+            stage_kv[3, unit] = vi_in[0, p, :, cols]
+
+    def kv_own(chunk):
+        for i in range(PER):
+            p, cols = place(chunk, i, core)
+            unit = chunk * PER + i
+            keys[unit, mine, :] = plain(kt_in[0, p, :, cols], kg[1:2])
+            keys[unit, mine_img, :] = roped(ki_in[0, p, :, cols], kg[0:1])
+            vals[unit, mine, :] = vt_in[0, p, :, cols]
+            vals[unit, mine_img, :] = vi_in[0, p, :, cols]
+
+    def exchange(sending):
+        rows, rows_img = (mine, mine_img) if sending else (theirs, theirs_img)
+        pairs = [
+            (stage_q, q_all.at[z, :, rows, :]),
+            (stage_kv.at[0], keys.at[:, rows, :]),
+            (stage_kv.at[1], keys.at[:, rows_img, :]),
+            (stage_kv.at[2], vals.at[:, rows, :]),
+            (stage_kv.at[3], vals.at[:, rows_img, :]),
+        ]
+        return [
+            remote(src, dst, ex_send.at[n], ex_recv.at[n], peer)
+            for n, (src, dst) in enumerate(pairs)
+        ]
+
+    def some(chunk):
+        return pl.ds(chunk * PER, PER)
+
+    def query_copy(to_right, owner, chunk):
+        block = q_all.at[owner, some(chunk)]
+        way = 1 if to_right else 0
+        return remote(
+            block, block, q_send.at[way, owner, chunk], q_recv.at[owner, chunk],
+            right if to_right else left,
+        )
+
+    def part_copies(to_right, owner, chunk):
+        way = 0 if to_right else 1
+        device = right if to_right else left
+        return (
+            remote(
+                out_part.at[owner, some(chunk)], in_part.at[way, owner, some(chunk)],
+                p_send.at[owner, chunk], p_recv.at[way, owner, chunk], device,
+            ),
+            remote(
+                out_lse.at[owner, chunk], in_lse.at[way, owner, chunk],
+                s_send.at[owner, chunk], s_recv.at[way, owner, chunk], device,
+            ),
+        )
+
+    def attend(owner, chunk):
+        live_text = tlen[prompt_of(chunk // 2)]
+        row = lax.broadcasted_iota(jnp.int32, (4 * ROWS, HD), 0)
+        live = (row >= 2 * ROWS) | (row + z * (2 * ROWS) < live_text)
+        for i in range(PER):
+            unit = chunk * PER + i
+            scores = lax.dot_general(
+                keys[unit], q_all[owner, unit], (((1,), (1,)), ((), ())),
+                preferred_element_type=F32,
+            ) * SCALE
+            scores = jnp.where(live, scores, -1e30)
+            top = jnp.max(scores, 0, keepdims=True)
+            expo = jnp.exp(scores - top)
+            total = jnp.sum(expo, 0, keepdims=True)
+            out = jnp.dot(vals_t[unit], expo.astype(BF16), preferred_element_type=F32)
+            part[owner, unit] = out / total
+            lse[owner, chunk, i : i + 1, :] = top + jnp.log(total)
+
+    def absorb(way, owner, chunk):
+        for copy in part_copies(way == 0, owner, chunk):
+            copy.wait_recv()
+        for i in range(PER):
+            unit = chunk * PER + i
+            here = lse[owner, chunk, i : i + 1, :]
+            there = in_lse[way, owner, chunk, i : i + 1, :]
+            top = jnp.maximum(here, there)
+            w_here = jnp.exp(here - top)
+            w_there = jnp.exp(there - top)
+            total = w_here + w_there
+            part[owner, unit] = part[owner, unit] * (w_here / total) + in_part[
+                way, owner, unit
+            ].astype(F32) * (w_there / total)
+            lse[owner, chunk, i : i + 1, :] = top + jnp.log(total)
+
+    def relay(to_right, owner, chunk):
+        if to_right:
+            pl.when(z > 0)(lambda: absorb(0, owner, chunk))
+        else:
+            pl.when(z < last)(lambda: absorb(1, owner, chunk))
+        out_part[owner, some(chunk)] = part[owner, some(chunk)].astype(BF16)
+        out_lse[owner, chunk] = lse[owner, chunk]
+        for copy in part_copies(to_right, owner, chunk):
+            copy.start()
+
+    def from_left(owner, chunk):
+        query_copy(True, owner, chunk).wait_recv()
+        pl.when(z < last)(lambda: query_copy(True, owner, chunk).start())
+
+    def from_right(owner, chunk):
+        query_copy(False, owner, chunk).wait_recv()
+        pl.when(z > 0)(lambda: query_copy(False, owner, chunk).start())
+
+    def attn_copy(chunk, sending):
+        first = (core if sending else other) * HEADS_CORE + (chunk % 2) * PER
+        return remote(
+            own_t.at[some(chunk), theirs, :], attn.at[chunk // 2, pl.ds(first, PER)],
+            a_send.at[chunk], a_recv.at[chunk], peer,
+        )
+
+    def conclude(chunk):
+        pl.when(z > 0)(lambda: absorb(0, z, chunk))
+        pl.when(z < last)(lambda: absorb(1, z, chunk))
+        for i in range(PER):
+            own_t[chunk * PER + i] = part[z, chunk * PER + i].T.astype(BF16)
+        attn_copy(chunk, True).start()
+        attn[chunk // 2, pl.ds(core * HEADS_CORE + (chunk % 2) * PER, PER)] = own_t[
+            some(chunk), mine, :
+        ]
+
+    tile = 256
+
+    def product(order, column):
+        rows = jnp.concatenate([attn[order, h] for h in range(2 * HEADS_CORE)], -1)
+        return jnp.dot(
+            rows, weight[:, pl.ds(pl.multiple_of(column, tile), tile)],
+            preferred_element_type=F32,
+        )
+
+    def y_copy(order, n):
+        return remote(
+            y_out.at[order, n], y_in.at[order, n], y_send.at[order, n], y_recv.at[order, n], y_peer
+        )
+
+    def project(order):
+        for chunk in (2 * order, 2 * order + 1):
+            attn_copy(chunk, False).wait_recv()
+        for n in range(2):
+            def send_tile(at, carry, n=n):
+                start = pl.multiple_of(at * tile, tile)
+                y_out[order, n, :, pl.ds(start, tile)] = product(
+                    order, (1 - b) * width + n * half + start
+                ).astype(BF16)
+                return carry
+
+            lax.fori_loop(0, half // tile, send_tile, 0)
+            y_copy(order, n).start()
+
+        def own_tile(at, carry):
+            start = pl.multiple_of(at * tile, tile)
+            proj[order, :, pl.ds(start, tile)] = product(order, b * width + start)
+            return carry
+
+        lax.fori_loop(0, width // tile, own_tile, 0)
+
+    def x_copy(n):
+        return remote(x_out.at[n], x_in.at[n], x_send.at[n], x_recv.at[n], x_peer)
+
+    def layer(order, n):
+        y_copy(order, n).wait_recv()
+        p = prompt_of(order)
+        cols = pl.ds(n * half, half)
+        summed = proj[order, :, cols] + y_in[order, n].astype(F32) + bias[:, cols]
+        return (
+            hid[0, p, :, cols].astype(F32) + gate[0, pl.ds(p, 1), cols] * summed
+        ).astype(BF16)
+
+    each_chunk(queries_for_peer)
+    pl.semaphore_wait(barrier, 3 + jnp.where(z > 0, 1, 0) + jnp.where(z < last, 1, 0))
+    sends = exchange(True)
+    arrivals = exchange(False)
+    sends[0].start()
+    each_chunk(queries_own)
+    arrivals[0].wait_recv()
+
+    def launch(chunk):
+        pl.when(z < last)(lambda: query_copy(True, z, chunk).start())
+        pl.when(z > 0)(lambda: query_copy(False, z, chunk).start())
+
+    each_chunk(launch)
+    each_chunk(kv_for_peer)
+    for copy in sends[1:]:
+        copy.start()
+    each_chunk(kv_own)
+    for copy in arrivals[1:]:
+        copy.wait_recv()
+
+    def turn_values(chunk):
+        for i in range(PER):
+            unit = chunk * PER + i
+            vals_t[unit] = vals[unit].astype(F32).T.astype(BF16)
+
+    each_chunk(turn_values)
+    each_chunk(lambda chunk: attend(z, chunk))
+
+    for step in range(1, CHIPS):
+        def at_step(chunk, step=step):
+            has_left = z >= step
+            has_right = z + step <= last
+            pl.when(has_left)(lambda: from_left(z - step, chunk))
+            pl.when(has_right)(lambda: from_right(z + step, chunk))
+            pl.when(has_left)(lambda: attend(z - step, chunk))
+            pl.when(has_right)(lambda: attend(z + step, chunk))
+            pl.when(step > z)(lambda: relay(True, step, chunk))
+            pl.when(last - step < z)(lambda: relay(False, last - step, chunk))
+            if step == last:
+                pl.when(chunk > 0)(lambda: conclude(chunk - 1))
+
+        each_chunk(at_step)
+
+    w_copy.wait()
+    project(0)
+    conclude(CHUNKS - 1)
+    for n in range(2):
+        x_out[n] = layer(0, n)
+        x_copy(n).start()
+    project(1)
+
+    moved = jnp.float32(0.0)
+    for i, size in enumerate(step_sizes()):
+        moved = jnp.where(sidx[0] == i, jnp.float32(size), moved)
+    amount = guidance[g]
+    for n in range(2):
+        cols = pl.ds(n * half, half)
+        own = layer(1, n).astype(F32)
+        x_copy(n).wait_recv()
+        got = x_in[n].astype(F32)
+        cond = jnp.where(g == 0, own, got)
+        uncond = jnp.where(g == 0, got, own)
+        guided = uncond + amount * (cond - uncond)
+        guided_o[0, :, cols] = guided.astype(BF16)
+        next_o[0, :, cols] = (latent[0, :, cols].astype(F32) + moved * guided).astype(BF16)
+
+    for copy in sends:
+        copy.wait_send()
+
+    def drain(chunk):
+        for owner in range(CHIPS):
+            pl.when((z >= owner) & (z < last))(lambda: query_copy(True, owner, chunk).wait_send())
+            pl.when((z <= owner) & (z > 0))(lambda: query_copy(False, owner, chunk).wait_send())
+
+            @pl.when(z != owner)
+            def _():
+                for copy in part_copies(True, owner, chunk):
+                    copy.wait_send()
+
+        attn_copy(chunk, True).wait_send()
+
+    each_chunk(drain)
+    for n in range(2):
+        y_copy(0, n).wait_send()
+        y_copy(1, n).wait_send()
+        x_copy(n).wait_send()
+
+
+def fused_shards(
+    img_hidden, img_query, img_key, img_value, txt_key, txt_value, query_gain, key_gain, gate,
+    proj_weight, proj_bias, guidance, text_len, step_index, latent,
+):
+    width = img_query.shape[3]
+    vmem = pl.BlockSpec(memory_space=pltpu.VMEM)
+    smem = pl.BlockSpec(memory_space=pltpu.SMEM)
+    away = pl.BlockSpec(memory_space=pl.ANY)
+    dma = pltpu.SemaphoreType.DMA
+    out = jax.ShapeDtypeStruct(latent.shape, BF16)
+    block = (UNITS, 2 * ROWS, HD)
+    return pl.pallas_call(
+        fused,
+        out_shape=(out, out),
+        in_specs=[vmem] * 9 + [away, vmem, smem, smem, smem, vmem, away, vmem],
+        out_specs=(vmem, vmem),
+        scratch_shapes=[
+            pltpu.VMEM(proj_weight.shape, BF16),
+            pltpu.VMEM((ROWS, 2 * HD), F32),
+            pltpu.VMEM((CHIPS,) + block, BF16),
+            pltpu.VMEM((UNITS, 4 * ROWS, HD), BF16),
+            pltpu.VMEM((UNITS, 4 * ROWS, HD), BF16),
+            pltpu.VMEM((UNITS, HD, 4 * ROWS), BF16),
+            pltpu.VMEM((UNITS, ROWS, HD), BF16),
+            pltpu.VMEM((4, UNITS, ROWS, HD), BF16),
+            pltpu.VMEM((CHIPS,) + block, F32),
+            pltpu.VMEM((CHIPS, CHUNKS, 8, HD), F32),
+            pltpu.VMEM((2, CHIPS) + block, BF16),
+            pltpu.VMEM((2, CHIPS, CHUNKS, 8, HD), F32),
+            pltpu.VMEM((CHIPS,) + block, BF16),
+            pltpu.VMEM((CHIPS, CHUNKS, 8, HD), F32),
+            pltpu.VMEM(block, BF16),
+            pltpu.VMEM((2, 2 * HEADS_CORE, ROWS, HD), BF16),
+            pltpu.VMEM((2, 2, ROWS, width // 2), BF16),
+            pltpu.VMEM((2, 2, ROWS, width // 2), BF16),
+            pltpu.VMEM((2, ROWS, width), F32),
+            pltpu.VMEM((2, ROWS, width // 2), BF16),
+            pltpu.VMEM((2, ROWS, width // 2), BF16),
+            dma, dma,
+            dma((5,)), dma((5,)),
+            dma((2, CHIPS, CHUNKS)), dma((CHIPS, CHUNKS)),
+            dma((CHIPS, CHUNKS)), dma((2, CHIPS, CHUNKS)),
+            dma((CHIPS, CHUNKS)), dma((2, CHIPS, CHUNKS)),
+            dma((CHUNKS,)), dma((CHUNKS,)),
+            dma((2, 2)), dma((2, 2)),
+            dma((2,)), dma((2,)),
+        ],
+        compiler_params=pltpu.CompilerParams(
+            collective_id=0, has_side_effects=True, vmem_limit_bytes=52 * 2**20
+        ),
+        name="fused_step",
+    )(
+        img_hidden, img_query, img_key, img_value, txt_key, txt_value,
+        query_gain.reshape(1, HD), key_gain, gate, proj_weight, proj_bias.reshape(1, width),
+        guidance, text_len, step_index, latent,
+        jnp.asarray(rope_table(2 * CHIPS)), jnp.asarray(swap_matrix(), BF16),
+    )
+
+
+def fits_fused(mesh):
+    return mesh.shape["seq"] == 2 * CHIPS and mesh.shape["blk"] == 2 and mesh.shape["guide"] == 2
+
+
 def solution(mesh):
     return jax.shard_map(
-        shards,
+        fused_shards if fits_fused(mesh) else shards,
         mesh=mesh,
         in_specs=(
             P("guide", None, "seq", "blk"),

time: 217 us -> 95.3 us (0.44)
  waiting for transfers between devices: 130 us -> 0 us
  Pallas kernels: 0 us -> 83.4 us
  other arithmetic: 28.7 us -> 0 us
  matrix products: 14.4 us -> 0 us
  local copies, waits for them, and re-layouts: 24 us -> 10.1 us
  between operations: 14.9 us -> 1.3 us
  starting transfers between devices: 3.77 us -> 0 us
    all_gather x2 -> x0, waiting for transfers between devices: 108 us -> none  [the longest x1 61 us: shards(): key_piece = lax.all_gather(keys_local, 'seq', axis=1, tiled=True)]
    pallas_call x0 -> x1, Pallas kernels: none -> 83.4 us  [fused_shards(): pl.pallas_call(fused, out_shape=(out, out), in_specs=[vmem] * 9 + [away,...]
    reduce_scatter x1 -> x0, waiting for transfers between devices: 15.8 us -> none  [shards(): lax.psum_scatter(partial_value.astype(jnp.bfloat16), 'blk', scatter_dimen...]
    dot_general x3 -> x0, matrix products: 14.4 us -> none  [the longest x1 7.21 us: shards(): jnp.einsum('pqhk,pkhd->pqhd', expo.astype(jnp.bfloat16), value_heads, pre...]
    all_gather x1 -> x0, local copies, waits for them, and re-layouts: 8.67 us -> none  [shards(): key_piece = lax.all_gather(keys_local, 'seq', axis=1, tiled=True)]
    another operation x4 -> x0, other arithmetic: 8.28 us -> none  [the longest x2 4.15 us: rotate(): return jnp.stack([first, second], -1).reshape(values.shape)]
    mul x5 -> x0, other arithmetic: 7.02 us -> none  [the longest x3 5.07 us: normed(): heads * heads]
    all_to_all x1 -> x0, waiting for transfers between devices: 5.46 us -> none  [shards(): lax.all_to_all(layer_out[None], 'guide', split_axis=1, concat_axis=0, til...]
  transfers between devices with their start and end apart: 4 -> 0, of which waited for: 4 -> 0; matrix products, arithmetic and copies ran while one was open for 10% -> 0% of each run, Pallas kernels for 0% -> 0%
where the time goes in v1:
time: 95.3 us; the launch traced here: 94.8 us
  Pallas kernels  83.4 us (88%)
  local copies, waits for them, and re-layouts  10.1 us (11%)
  between operations  1.3 us (1%)
    pallas_call x1, Pallas kernels, fused_shards(): pl.pallas_call(fused, out_shape=(out, out), in_specs=[vmem] * 9 + [away,...  83.4 us
    unnamed x22, local copies, waits for them, and re-layouts  9.37 us

profile of v1, /device:TPU:0, one launch (start us, length us, event | category | flops | bytes accessed | tf_op | source)
XLA Modules:
  0.0 94.8 jit_solution(12904860094577085380)
XLA Ops:
  1.3 0.7 reshape.11.bias
  2.0 0.0 copy-start
  2.0 1.0 %copy-done = bf16[1,2,64,1536]{3,2,1,0:T(8,128)(2,1)S(1)} copy-done((bf16[1,2,64,1536]{3,2,1,0:T(8,128)(2,1)S(1)}, bf16[1,2,64,1536]{3,2,1,0:T(8,128)(2,1)}, u32[]{:S(2)}) %copy-start) | copy-done | bytes 393240
  3.0 0.0 copy-start.1
  3.0 1.0 %copy-done.1 = bf16[1,2,64,1536]{3,2,1,0:T(8,128)(2,1)S(1)} copy-done((bf16[1,2,64,1536]{3,2,1,0:T(8,128)(2,1)S(1)}, bf16[1,2,64,1536]{3,2,1,0:T(8,128)(2,1)}, u32[]{:S(2)}) %copy-start.1) | copy-done | bytes 393240
  4.0 0.0 copy-start.2
  4.0 1.0 %copy-done.2 = bf16[1,2,64,1536]{3,2,1,0:T(8,128)(2,1)S(1)} copy-done((bf16[1,2,64,1536]{3,2,1,0:T(8,128)(2,1)S(1)}, bf16[1,2,64,1536]{3,2,1,0:T(8,128)(2,1)}, u32[]{:S(2)}) %copy-start.2) | copy-done | bytes 393240
  5.0 0.0 copy-start.3
  5.0 0.9 copy-done.3
  5.9 0.0 copy-start.4
  5.9 0.8 copy-done.4
  6.7 0.0 copy-start.5
  6.7 0.7 copy-done.5
  7.4 0.0 copy-start.6
  7.4 0.7 copy-done.6
  8.0 0.0 copy-start.7
  8.0 0.7 copy-done.7
  8.7 0.0 copy-start.8
  8.7 0.7 copy-done.8
  9.4 0.0 copy-start.9
  9.4 0.7 copy-done.9
  10.0 83.4 %fused_step.1 = (bf16[1,64,1536]{2,1,0:T(8,128)(2,1)S(1)}, bf16[1,64,1536]{2,1,0:T(8,128)(2,1)S(1)}) custom-call(bf16[1,2,64,1536]{3,2,1,0:T(8,128)(2,1)S(1)} %copy-done, bf16[1,2,64,1536]{3,2,1,0:T(8,128)(2,1)S(1)} %copy-done.1, bf16[1,2,64,1536]{3,2,1,0:T(8,128)(2,1)S(1)} %copy-done.2, bf16[1,2,64,1536]{3,2,1,0:T(8,128)(2,1)} %vi_in.1, ...), custom_call_target="tpu_custom_call" | custom-call | tf_op jit(solution)/shard_map/fused_step/pallas_call | solution.py:531
  93.4 0.7 copy.22
  94.1 0.7 copy.23
Async XLA Ops:
  2.0 1.0 %copy-start = (bf16[1,2,64,1536]{3,2,1,0:T(8,128)(2,1)S(1)}, bf16[1,2,64,1536]{3,2,1,0:T(8,128)(2,1)}, u32[]{:S(2)}) copy-start(bf16[1,2,64,1536]{3,2,1,0:T(8,128)(2,1)} %hid.1) | copy-start | bytes 1179652
  3.0 1.0 %copy-start.1 = (bf16[1,2,64,1536]{3,2,1,0:T(8,128)(2,1)S(1)}, bf16[1,2,64,1536]{3,2,1,0:T(8,128)(2,1)}, u32[]{:S(2)}) copy-start(bf16[1,2,64,1536]{3,2,1,0:T(8,128)(2,1)} %q_in.1) | copy-start | bytes 1179652
  4.0 1.0 %copy-start.2 = (bf16[1,2,64,1536]{3,2,1,0:T(8,128)(2,1)S(1)}, bf16[1,2,64,1536]{3,2,1,0:T(8,128)(2,1)}, u32[]{:S(2)}) copy-start(bf16[1,2,64,1536]{3,2,1,0:T(8,128)(2,1)} %ki_in.1) | copy-start | bytes 1179652
  5.0 0.9 copy-start.3
  5.9 0.8 copy-start.4
  6.7 0.7 copy-start.5
  7.4 0.7 copy-start.6
  8.0 0.7 copy-start.7
  8.7 0.7 copy-start.8
  9.4 0.7 copy-start.9

commit v2 on v1

--- a/solution.py
+++ b/solution.py
@@ -125,6 +125,7 @@
 UNITS = CHUNKS * PER
 HEADS_CORE = 6
 SCALE = HD ** (-0.5)
+SCALE2 = SCALE * float(np.log2(np.e))
 F32 = jnp.float32
 BF16 = jnp.bfloat16
 
@@ -159,8 +160,9 @@
 
 
 def fused(
-    hid, q_in, ki_in, vi_in, kt_in, vt_in, qg, kg, gate, w_hbm, bias, guidance, tlen, sidx, latent,
-    rope_hbm, perm, guided_o, next_o,
+    hid_hbm, q_hbm, ki_hbm, vi_hbm, kt_hbm, vt_hbm, qg_hbm, kg_hbm, gate_hbm, w_hbm, bias_hbm,
+    guidance, tlen, sidx, latent_hbm, rope_hbm, perm_hbm, guided_o, next_o,
+    hid, q_in, ki_in, vi_in, kt_in, vt_in, qg, kg, gate, bias, latent, perm, load_sem,
     weight, rope, q_all, keys, vals, vals_t, stage_q, stage_kv, part, lse, in_part, in_lse,
     out_part, out_lse, own_t, attn, y_out, y_in, proj, x_out, x_in,
     w_sem, rope_sem, ex_send, ex_recv, q_send, q_recv, p_send, p_recv, s_send, s_recv,
@@ -201,11 +203,23 @@
     pl.when(z > 0)(lambda: greet(left))
     pl.when(z < last)(lambda: greet(right))
 
+    rope_copy = pltpu.make_async_copy(rope_hbm.at[s], rope, rope_sem)
+    rope_copy.start()
+    loads = [
+        pltpu.make_async_copy(src, dst, load_sem.at[n])
+        for n, (src, dst) in enumerate([
+            (q_hbm, q_in), (qg_hbm, qg), (perm_hbm, perm),
+            (kt_hbm, kt_in), (ki_hbm, ki_in), (kg_hbm, kg), (vt_hbm, vt_in), (vi_hbm, vi_in),
+            (hid_hbm, hid), (gate_hbm, gate), (bias_hbm, bias), (latent_hbm, latent),
+        ])
+    ]
+    for load in loads:
+        load.start()
     w_copy = pltpu.make_async_copy(w_hbm, weight, w_sem)
     w_copy.start()
-    rope_copy = pltpu.make_async_copy(rope_hbm.at[s], rope, rope_sem)
-    rope_copy.start()
     rope_copy.wait()
+    for load in loads[:3]:
+        load.wait()
 
     lane = lax.broadcasted_iota(jnp.int32, (8, HD), 1)
 
@@ -315,21 +329,30 @@
 
     def attend(owner, chunk):
         live_text = tlen[prompt_of(chunk // 2)]
-        row = lax.broadcasted_iota(jnp.int32, (4 * ROWS, HD), 0)
-        live = (row >= 2 * ROWS) | (row + z * (2 * ROWS) < live_text)
-        for i in range(PER):
-            unit = chunk * PER + i
-            scores = lax.dot_general(
+        row = lax.broadcasted_iota(jnp.int32, (2 * ROWS, HD), 0)
+        live = row + z * (2 * ROWS) < live_text
+        units = [chunk * PER + i for i in range(PER)]
+        scores = [
+            lax.dot_general(
                 keys[unit], q_all[owner, unit], (((1,), (1,)), ((), ())),
                 preferred_element_type=F32,
-            ) * SCALE
-            scores = jnp.where(live, scores, -1e30)
-            top = jnp.max(scores, 0, keepdims=True)
-            expo = jnp.exp(scores - top)
-            total = jnp.sum(expo, 0, keepdims=True)
-            out = jnp.dot(vals_t[unit], expo.astype(BF16), preferred_element_type=F32)
-            part[owner, unit] = out / total
-            lse[owner, chunk, i : i + 1, :] = top + jnp.log(total)
+            )
+            for unit in units
+        ]
+        scores = [
+            jnp.concatenate([jnp.where(live, raw[: 2 * ROWS], -1e30), raw[2 * ROWS :]], 0)
+            for raw in scores
+        ]
+        tops = [jnp.max(raw, 0, keepdims=True) for raw in scores]
+        expos = [jnp.exp2((raw - top) * SCALE2) for raw, top in zip(scores, tops)]
+        totals = [jnp.sum(expo, 0, keepdims=True) for expo in expos]
+        outs = [
+            jnp.dot(vals_t[unit], expo.astype(BF16), preferred_element_type=F32)
+            for unit, expo in zip(units, expos)
+        ]
+        for i in range(PER):
+            part[owner, units[i]] = outs[i] * (1.0 / totals[i])
+            lse[owner, chunk, i : i + 1, :] = tops[i] * SCALE + jnp.log(totals[i])
 
     def absorb(way, owner, chunk):
         for copy in part_copies(way == 0, owner, chunk):
@@ -442,6 +465,8 @@
         pl.when(z > 0)(lambda: query_copy(False, z, chunk).start())
 
     each_chunk(launch)
+    for load in loads[3:8]:
+        load.wait()
     each_chunk(kv_for_peer)
     for copy in sends[1:]:
         copy.start()
@@ -455,7 +480,7 @@
             vals_t[unit] = vals[unit].astype(F32).T.astype(BF16)
 
     each_chunk(turn_values)
-    each_chunk(lambda chunk: attend(z, chunk))
+    at_end = (z == 0) | (z == last)
 
     for step in range(1, CHIPS):
         def at_step(chunk, step=step):
@@ -467,11 +492,16 @@
             pl.when(has_right)(lambda: attend(z + step, chunk))
             pl.when(step > z)(lambda: relay(True, step, chunk))
             pl.when(last - step < z)(lambda: relay(False, last - step, chunk))
+            if step == 1:
+                pl.when(at_end)(lambda: attend(z, chunk))
             if step == last:
+                pl.when(jnp.logical_not(at_end))(lambda: attend(z, chunk))
                 pl.when(chunk > 0)(lambda: conclude(chunk - 1))
 
         each_chunk(at_step)
 
+    for load in loads[8:]:
+        load.wait()
     w_copy.wait()
     project(0)
     conclude(CHUNKS - 1)
@@ -524,16 +554,24 @@
     width = img_query.shape[3]
     vmem = pl.BlockSpec(memory_space=pltpu.VMEM)
     smem = pl.BlockSpec(memory_space=pltpu.SMEM)
-    away = pl.BlockSpec(memory_space=pl.ANY)
+    away = pl.BlockSpec(memory_space=pltpu.HBM)
     dma = pltpu.SemaphoreType.DMA
     out = jax.ShapeDtypeStruct(latent.shape, BF16)
     block = (UNITS, 2 * ROWS, HD)
     return pl.pallas_call(
         fused,
         out_shape=(out, out),
-        in_specs=[vmem] * 9 + [away, vmem, smem, smem, smem, vmem, away, vmem],
+        in_specs=[away] * 11 + [smem] * 3 + [away] * 3,
         out_specs=(vmem, vmem),
         scratch_shapes=[
+            *[pltpu.VMEM(img_query.shape, BF16)] * 6,
+            pltpu.VMEM((1, HD), F32),
+            pltpu.VMEM((2, HD), F32),
+            pltpu.VMEM(gate.shape, F32),
+            pltpu.VMEM((1, width), F32),
+            pltpu.VMEM(latent.shape, BF16),
+            pltpu.VMEM((HD, HD), BF16),
+            dma((12,)),
             pltpu.VMEM(proj_weight.shape, BF16),
             pltpu.VMEM((ROWS, 2 * HD), F32),
             pltpu.VMEM((CHIPS,) + block, BF16),
@@ -565,7 +603,7 @@
             dma((2,)), dma((2,)),
         ],
         compiler_params=pltpu.CompilerParams(
-            collective_id=0, has_side_effects=True, vmem_limit_bytes=52 * 2**20
+            collective_id=0, has_side_effects=True, vmem_limit_bytes=60 * 2**20
         ),
         name="fused_step",
     )(

time: 95.3 us -> 88.8 us (0.932)
  local copies, waits for them, and re-layouts: 10.1 us -> 4.53 us
    unnamed x22 -> x2, local copies, waits for them, and re-layouts: 9.37 us -> 3.23 us
where the time goes in v2:
time: 88.8 us; the launch traced here: 88.5 us
  Pallas kernels  82.7 us (93%)
  local copies, waits for them, and re-layouts  4.53 us (5%)
  between operations  1.29 us (1%)
    pallas_call x1, Pallas kernels, fused_shards(): pl.pallas_call(fused, out_shape=(out, out), in_specs=[away] * 11 + [smem]...  82.7 us
    unnamed x2, local copies, waits for them, and re-layouts  3.23 us

profile of v2, /device:TPU:0, one launch (start us, length us, event | category | flops | bytes accessed | tf_op | source)
XLA Modules:
  0.0 88.5 jit_solution(15394966138932928114)
XLA Ops:
  1.3 1.3 %reshape.11.bias_hbm = f32[1,1536]{1,0:T(1,128)} reshape(f32[1536]{0:T(1024)} %param.27) | data formatting | bytes 12288 | tf_op jit(solution)/shard_map/reshape | solution.py:611
  2.6 82.7 %fused_step.1 = (bf16[1,64,1536]{2,1,0:T(8,128)(2,1)}, bf16[1,64,1536]{2,1,0:T(8,128)(2,1)}) custom-call(bf16[1,2,64,1536]{3,2,1,0:T(8,128)(2,1)} %hid_hbm.1, bf16[1,2,64,1536]{3,2,1,0:T(8,128)(2,1)} %q_hbm.1, bf16[1,2,64,1536]{3,2,1,0:T(8,128)(2,1)} %ki_hbm.1, bf16[1,2,64,1536]{3,2,1,0:T(8,128)(2,1)} %vi_hbm.1, bf16[1,2,64,1536]{3,2,1,0:T(8,128)(2,1)} %kt_hbm.1, ...), custom_call_target="tpu_custom_call" | custom-call | tf_op jit(solution)/shard_map/fused_step/pallas_call | solution.py:561
  85.3 1.6 %copy.22 = bf16[1,64,1536]{2,1,0:T(8,128)(2,1)} copy(bf16[1,64,1536]{2,1,0:T(8,128)(2,1)} %get-tuple-element.4) | data formatting | bytes 393216
  86.9 1.6 %copy.23 = bf16[1,64,1536]{2,1,0:T(8,128)(2,1)} copy(bf16[1,64,1536]{2,1,0:T(8,128)(2,1)} %get-tuple-element.5) | data formatting | bytes 393216

commit v3 on v2

--- a/solution.py
+++ b/solution.py
@@ -151,18 +151,10 @@
     return out
 
 
-def step_sizes():
-    def sigma(i):
-        u = 1.0 - i / STEPS
-        return 3.0 * u / (1.0 + 2.0 * u)
-
-    return [sigma(i + 1) - sigma(i) for i in range(STEPS)]
-
-
 def fused(
     hid_hbm, q_hbm, ki_hbm, vi_hbm, kt_hbm, vt_hbm, qg_hbm, kg_hbm, gate_hbm, w_hbm, bias_hbm,
-    guidance, tlen, sidx, latent_hbm, rope_hbm, perm_hbm, guided_o, next_o,
-    hid, q_in, ki_in, vi_in, kt_in, vt_in, qg, kg, gate, bias, latent, perm, load_sem,
+    guidance, tlen, rope_hbm, perm_hbm, guided_o,
+    hid, q_in, ki_in, vi_in, kt_in, vt_in, qg, kg, gate, bias, perm, load_sem,
     weight, rope, q_all, keys, vals, vals_t, stage_q, stage_kv, part, lse, in_part, in_lse,
     out_part, out_lse, own_t, attn, y_out, y_in, proj, x_out, x_in,
     w_sem, rope_sem, ex_send, ex_recv, q_send, q_recv, p_send, p_recv, s_send, s_recv,
@@ -210,7 +202,7 @@
         for n, (src, dst) in enumerate([
             (q_hbm, q_in), (qg_hbm, qg), (perm_hbm, perm),
             (kt_hbm, kt_in), (ki_hbm, ki_in), (kg_hbm, kg), (vt_hbm, vt_in), (vi_hbm, vi_in),
-            (hid_hbm, hid), (gate_hbm, gate), (bias_hbm, bias), (latent_hbm, latent),
+            (hid_hbm, hid), (gate_hbm, gate), (bias_hbm, bias),
         ])
     ]
     for load in loads:
@@ -471,27 +463,33 @@
     for copy in sends[1:]:
         copy.start()
     each_chunk(kv_own)
+
+    def turn_values(chunk):
+        for i in range(PER):
+            unit = chunk * PER + i
+            vals_t[unit] = vals[unit].astype(F32).T.astype(BF16)
+
+    at_end = (z == 0) | (z == last)
+
+    def forward(step, chunk):
+        pl.when(z >= step)(lambda: from_left(z - step, chunk))
+        pl.when(z + step <= last)(lambda: from_right(z + step, chunk))
+
+    each_chunk(lambda chunk: forward(1, chunk))
     for copy in arrivals[1:]:
         copy.wait_recv()
-
-    def turn_values(chunk):
-        for i in range(PER):
-            unit = chunk * PER + i
-            vals_t[unit] = vals[unit].astype(F32).T.astype(BF16)
-
     each_chunk(turn_values)
-    at_end = (z == 0) | (z == last)
 
     for step in range(1, CHIPS):
         def at_step(chunk, step=step):
             has_left = z >= step
             has_right = z + step <= last
-            pl.when(has_left)(lambda: from_left(z - step, chunk))
-            pl.when(has_right)(lambda: from_right(z + step, chunk))
             pl.when(has_left)(lambda: attend(z - step, chunk))
             pl.when(has_right)(lambda: attend(z + step, chunk))
             pl.when(step > z)(lambda: relay(True, step, chunk))
             pl.when(last - step < z)(lambda: relay(False, last - step, chunk))
+            if step < last:
+                forward(step + 1, chunk)
             if step == 1:
                 pl.when(at_end)(lambda: attend(z, chunk))
             if step == last:
@@ -510,9 +508,6 @@
         x_copy(n).start()
     project(1)
 
-    moved = jnp.float32(0.0)
-    for i, size in enumerate(step_sizes()):
-        moved = jnp.where(sidx[0] == i, jnp.float32(size), moved)
     amount = guidance[g]
     for n in range(2):
         cols = pl.ds(n * half, half)
@@ -521,9 +516,7 @@
         got = x_in[n].astype(F32)
         cond = jnp.where(g == 0, own, got)
         uncond = jnp.where(g == 0, got, own)
-        guided = uncond + amount * (cond - uncond)
-        guided_o[0, :, cols] = guided.astype(BF16)
-        next_o[0, :, cols] = (latent[0, :, cols].astype(F32) + moved * guided).astype(BF16)
+        guided_o[0, :, cols] = uncond + amount * (cond - uncond)
 
     for copy in sends:
         copy.wait_send()
@@ -556,22 +549,20 @@
     smem = pl.BlockSpec(memory_space=pltpu.SMEM)
     away = pl.BlockSpec(memory_space=pltpu.HBM)
     dma = pltpu.SemaphoreType.DMA
-    out = jax.ShapeDtypeStruct(latent.shape, BF16)
     block = (UNITS, 2 * ROWS, HD)
-    return pl.pallas_call(
+    guided_f = pl.pallas_call(
         fused,
-        out_shape=(out, out),
-        in_specs=[away] * 11 + [smem] * 3 + [away] * 3,
-        out_specs=(vmem, vmem),
+        out_shape=jax.ShapeDtypeStruct(latent.shape, F32),
+        in_specs=[away] * 11 + [smem] * 2 + [away] * 2,
+        out_specs=vmem,
         scratch_shapes=[
             *[pltpu.VMEM(img_query.shape, BF16)] * 6,
             pltpu.VMEM((1, HD), F32),
             pltpu.VMEM((2, HD), F32),
             pltpu.VMEM(gate.shape, F32),
             pltpu.VMEM((1, width), F32),
-            pltpu.VMEM(latent.shape, BF16),
             pltpu.VMEM((HD, HD), BF16),
-            dma((12,)),
+            dma((11,)),
             pltpu.VMEM(proj_weight.shape, BF16),
             pltpu.VMEM((ROWS, 2 * HD), F32),
             pltpu.VMEM((CHIPS,) + block, BF16),
@@ -609,9 +600,15 @@
     )(
         img_hidden, img_query, img_key, img_value, txt_key, txt_value,
         query_gain.reshape(1, HD), key_gain, gate, proj_weight, proj_bias.reshape(1, width),
-        guidance, text_len, step_index, latent,
+        guidance, text_len,
         jnp.asarray(rope_table(2 * CHIPS)), jnp.asarray(swap_matrix(), BF16),
     )
+    index = step_index[0]
+    u_now = 1.0 - index.astype(F32) / STEPS
+    u_next = 1.0 - (index + 1).astype(F32) / STEPS
+    step_size = 3.0 * u_next / (1.0 + 2.0 * u_next) - 3.0 * u_now / (1.0 + 2.0 * u_now)
+    next_state = (latent.astype(F32) + step_size * guided_f).astype(BF16)
+    return (guided_f.astype(BF16), next_state)
 
 
 def fits_fused(mesh):

time: 88.8 us -> 91 us (1.025)
  Pallas kernels: 82.7 us -> 86.2 us
  local copies, waits for them, and re-layouts: 4.53 us -> 1.3 us
  other arithmetic: 0 us -> 1.91 us
    pallas_call x1, Pallas kernels: 82.7 us -> 86.2 us  [fused_shards(): pl.pallas_call(fused, out_shape=jax.ShapeDtypeStruct(latent.shape, F32),...]
    unnamed x2, local copies, waits for them, and re-layouts: 3.23 us -> 0.01 us
    convert_element_type x0 -> x1, other arithmetic: none -> 1.91 us  [fused_shards(): next_state = (latent.astype(F32) + step_size * guided_f).astype(BF16)]
where the time goes in v3:
time: 91 us; the launch traced here: 90.8 us
  Pallas kernels  86.2 us (95%)
  other arithmetic  1.91 us (2%)
  between operations  1.43 us (2%)
  local copies, waits for them, and re-layouts  1.3 us (1%)
    pallas_call x1, Pallas kernels, fused_shards(): pl.pallas_call(fused, out_shape=jax.ShapeDtypeStruct(latent.shape, F32),...  86.2 us
    convert_element_type x1, other arithmetic, fused_shards(): next_state = (latent.astype(F32) + step_size * guided_f).astype(BF16)  1.91 us

profile of v3, /device:TPU:0, one launch (start us, length us, event | category | flops | bytes accessed | tf_op | source)
XLA Modules:
  0.0 90.8 jit_solution(1257812951370838282)
XLA Ops:
  0.6 0.0 copy-start
  1.4 1.3 %reshape.27.bias_hbm = f32[1,1536]{1,0:T(1,128)} reshape(f32[1536]{0:T(1024)} %param.27) | data formatting | bytes 12288 | tf_op jit(solution)/shard_map/reshape | solution.py:602
  2.7 86.2 %fused_step.1 = f32[1,64,1536]{2,1,0:T(8,128)} custom-call(bf16[1,2,64,1536]{3,2,1,0:T(8,128)(2,1)} %hid_hbm.1, bf16[1,2,64,1536]{3,2,1,0:T(8,128)(2,1)} %q_hbm.1, bf16[1,2,64,1536]{3,2,1,0:T(8,128)(2,1)} %ki_hbm.1, bf16[1,2,64,1536]{3,2,1,0:T(8,128)(2,1)} %vi_hbm.1, bf16[1,2,64,1536]{3,2,1,0:T(8,128)(2,1)} %kt_hbm.1, bf16[1,2,64,1536]{3,2,1,0:T(8,128)(2,1)} %vt_hbm.1, ...), custom_call_target="tpu_custom_call" | custom-call | tf_op jit(solution)/shard_map/fused_step/pallas_call | solution.py:553
  88.9 0.0 copy-done
  88.9 1.9 %add_convert_fusion = (bf16[1,64,1536]{2,1,0:T(8,128)(2,1)}, bf16[1,64,1536]{2,1,0:T(8,128)(2,1)}) fusion(f32[1,64,1536]{2,1,0:T(8,128)} %fused_step.1, bf16[1,64,1536]{2,1,0:T(8,128)(2,1)S(1)} %copy-done, f32[]{:T(128)} %bitcast.1), kind=kLoop, calls=%fused_computation | loop fusion | flops 491520 | bytes 983044 | tf_op jit(solution)/shard_map/convert_element_type | solution.py:610
Async XLA Ops:
  0.6 88.3 %copy-start = (bf16[1,64,1536]{2,1,0:T(8,128)(2,1)S(1)}, bf16[1,64,1536]{2,1,0:T(8,128)(2,1)}, u32[]{:S(2)}) copy-start(bf16[1,64,1536]{2,1,0:T(8,128)(2,1)} %param.31) | copy-start | bytes 589828

commit v4 on v3

--- a/solution.py
+++ b/solution.py
@@ -463,33 +463,27 @@
     for copy in sends[1:]:
         copy.start()
     each_chunk(kv_own)
+    for copy in arrivals[1:]:
+        copy.wait_recv()
 
     def turn_values(chunk):
         for i in range(PER):
             unit = chunk * PER + i
             vals_t[unit] = vals[unit].astype(F32).T.astype(BF16)
 
+    each_chunk(turn_values)
     at_end = (z == 0) | (z == last)
-
-    def forward(step, chunk):
-        pl.when(z >= step)(lambda: from_left(z - step, chunk))
-        pl.when(z + step <= last)(lambda: from_right(z + step, chunk))
-
-    each_chunk(lambda chunk: forward(1, chunk))
-    for copy in arrivals[1:]:
-        copy.wait_recv()
-    each_chunk(turn_values)
 
     for step in range(1, CHIPS):
         def at_step(chunk, step=step):
             has_left = z >= step
             has_right = z + step <= last
+            pl.when(has_left)(lambda: from_left(z - step, chunk))
+            pl.when(has_right)(lambda: from_right(z + step, chunk))
             pl.when(has_left)(lambda: attend(z - step, chunk))
             pl.when(has_right)(lambda: attend(z + step, chunk))
             pl.when(step > z)(lambda: relay(True, step, chunk))
             pl.when(last - step < z)(lambda: relay(False, last - step, chunk))
-            if step < last:
-                forward(step + 1, chunk)
             if step == 1:
                 pl.when(at_end)(lambda: attend(z, chunk))
             if step == last:

time: 91 us -> 87.7 us (0.964)
  Pallas kernels: 86.2 us -> 82.8 us
    pallas_call x1, Pallas kernels: 86.2 us -> 82.8 us  [fused_shards(): pl.pallas_call(fused, out_shape=jax.ShapeDtypeStruct(latent.shape, F32),...]
where the time goes in v4:
time: 87.7 us; the launch traced here: 87.5 us
  Pallas kernels  82.8 us (94%)
  other arithmetic  1.91 us (2%)
  between operations  1.43 us (2%)
  local copies, waits for them, and re-layouts  1.3 us (1%)
    pallas_call x1, Pallas kernels, fused_shards(): pl.pallas_call(fused, out_shape=jax.ShapeDtypeStruct(latent.shape, F32),...  82.8 us
    convert_element_type x1, other arithmetic, fused_shards(): next_state = (latent.astype(F32) + step_size * guided_f).astype(BF16)  1.91 us

profile of v4, /device:TPU:0, one launch (start us, length us, event | category | flops | bytes accessed | tf_op | source)
XLA Modules:
  0.0 87.5 jit_solution(2071078255011611504)
XLA Ops:
  0.6 0.0 copy-start
  1.4 1.3 %reshape.27.bias_hbm = f32[1,1536]{1,0:T(1,128)} reshape(f32[1536]{0:T(1024)} %param.27) | data formatting | bytes 12288 | tf_op jit(solution)/shard_map/reshape | solution.py:596
  2.7 82.8 %fused_step.1 = f32[1,64,1536]{2,1,0:T(8,128)} custom-call(bf16[1,2,64,1536]{3,2,1,0:T(8,128)(2,1)} %hid_hbm.1, bf16[1,2,64,1536]{3,2,1,0:T(8,128)(2,1)} %q_hbm.1, bf16[1,2,64,1536]{3,2,1,0:T(8,128)(2,1)} %ki_hbm.1, bf16[1,2,64,1536]{3,2,1,0:T(8,128)(2,1)} %vi_hbm.1, bf16[1,2,64,1536]{3,2,1,0:T(8,128)(2,1)} %kt_hbm.1, bf16[1,2,64,1536]{3,2,1,0:T(8,128)(2,1)} %vt_hbm.1, ...), custom_call_target="tpu_custom_call" | custom-call | tf_op jit(solution)/shard_map/fused_step/pallas_call | solution.py:547
  85.5 0.0 copy-done
  85.5 1.9 %add_convert_fusion = (bf16[1,64,1536]{2,1,0:T(8,128)(2,1)}, bf16[1,64,1536]{2,1,0:T(8,128)(2,1)}) fusion(f32[1,64,1536]{2,1,0:T(8,128)} %fused_step.1, bf16[1,64,1536]{2,1,0:T(8,128)(2,1)S(1)} %copy-done, f32[]{:T(128)} %bitcast.1), kind=kLoop, calls=%fused_computation | loop fusion | flops 491520 | bytes 983044 | tf_op jit(solution)/shard_map/convert_element_type | solution.py:604
Async XLA Ops:
  0.6 84.9 %copy-start = (bf16[1,64,1536]{2,1,0:T(8,128)(2,1)S(1)}, bf16[1,64,1536]{2,1,0:T(8,128)(2,1)}, u32[]{:S(2)}) copy-start(bf16[1,64,1536]{2,1,0:T(8,128)(2,1)} %param.31) | copy-start | bytes 589828
